TPU v7x, 32 devices: a whole 2x2x4 slice. The times are simulated.
32 devices in a mesh: docs: 16 (over z, x, core), dims: 2 (over y).
Axes of the slice: x: 2, y: 2, z: 4, core: 2. Of those that a mesh axis runs over, the one named last changes fastest.
Arguments:
- queries: bfloat16 [8192, 3072], P('docs', 'dims'), may hold values from -6 to 6
- doc_vectors: bfloat16 [32768, 3072], P('docs', 'dims'), may hold values from -6 to 6
- surv_pairs: int32 [16, 144], P('docs'), may hold values from 0 to 1023
- surv_count: int32 [16], P('docs'), may hold values from 36 to 144, as said below
- short_pairs: int32 [16, 96], P('docs'), may hold values from 0 to 1023
- short_count: int32 [16], P('docs'), may hold values from 24 to 96, as said below
Outputs:
- prefix_scores: float32 [16, 144, 128, 128], P('docs', None, 'dims')
- full_scores: float32 [16, 96, 128, 128], P('docs', None, 'dims')
Inputs may be any that keep to these rules, and one draw needn't show every extreme that they name: `surv_count`: each shard's live survivor slots; some shard has all 144 slots live. `short_count`: each shard's live shortlist slots; some shard has all 96 slots live.
All inputs are finite; a program needn't handle non-finite values.
Results may differ from a plain program's by a relative error of at most 0.0003.
Values may be sent and summed in bfloat16 or wider, within the bound.
A program may use at most 256 MiB of HBM per device.

v0:
```python
import jax
import jax.numpy as jnp
from jax import lax
from jax.sharding import PartitionSpec as P

D = 3072
PREFIX = 768
QB = 128
DB = 128


def shards(queries, doc_vectors, surv_pairs, surv_count, short_pairs, short_count):
    every_query = lax.all_gather(queries, "docs", axis=0, tiled=True)
    slice_width = queries.shape[1]
    query_blocks = every_query.reshape(-1, QB, slice_width)
    doc_blocks = doc_vectors.reshape(-1, DB, slice_width)
    local_blocks = doc_blocks.shape[0]
    columns = lax.axis_index("dims") * slice_width + jnp.arange(slice_width)
    prefix_blocks = jnp.where(
        columns[None, None, :] < PREFIX, doc_blocks, jnp.zeros((), doc_blocks.dtype)
    )

    def pair_products(pair_ids, doc_side):
        picked_queries = jnp.take(query_blocks, pair_ids // local_blocks, axis=0)
        picked_docs = jnp.take(doc_side, pair_ids % local_blocks, axis=0)
        return jnp.einsum(
            "gqc,gdc->gqd", picked_queries, picked_docs, preferred_element_type=jnp.float32
        )

    def score_slots(pair_list, doc_side):
        return pair_products(pair_list, doc_side)

    full_terms = score_slots(short_pairs[0], doc_blocks)
    prefix_terms = score_slots(surv_pairs[0], prefix_blocks)
    prefix_sum, full_sum = (
        lax.psum_scatter(prefix_terms, "dims", scatter_dimension=1, tiled=True),
        lax.psum_scatter(full_terms, "dims", scatter_dimension=1, tiled=True),
    )

    def finish(summed, live_count, factor):
        slots = jnp.arange(summed.shape[0])
        return jnp.where(slots[:, None, None] < live_count, summed * factor, jnp.float32(0.0))

    prefix_out = finish(prefix_sum, surv_count[0], float(PREFIX) ** (-0.5))
    full_out = finish(full_sum, short_count[0], float(D) ** (-0.5))
    return (prefix_out[None], full_out[None])


def solution(mesh):
    placed = (
        P("docs", "dims"),
        P("docs", "dims"),
        P("docs", None),
        P("docs"),
        P("docs", None),
        P("docs"),
    )
    return jax.shard_map(
        shards,
        mesh=mesh,
        in_specs=placed,
        out_specs=(P("docs", None, "dims", None), P("docs", None, "dims", None)),
        check_vma=False,
    )
```

profile of v0, /device:TPU:0, one launch (start us, length us, event | category | flops | bytes accessed | tf_op | source)
XLA Modules:
  0.0 413.4 jit_solution(7248077300480599414)
XLA Ops:
  7.2 0.0 all-gather.2.cloned.1.call-start
  7.2 0.7 all-gather.2.cloned.1.call-update
  7.9 0.0 reduce-scatter.5.cloned.1.call-start
  7.9 0.7 fusion.12
  8.6 0.0 copy-start.1
  8.6 17.8 %gather_fusion.3 = bf16[96,128,1536]{2,1,0:T(8,128)(2,1)} fusion(bf16[16,128,1536]{2,1,0:T(8,128)(2,1)} %bitcast.67, s32[1024]{0:T(1024)S(1)} %get-tuple-element.10), kind=kCustom, calls=%fused_computation.3 | custom fusion | bytes 75497856 | tf_op jit(solution)/shard_map/jit(_take)/gather | solution.py:25
  26.4 0.0 copy-done.1
  26.4 114.5 %all-gather.2.cloned.1.call-done = bf16[8192,1536]{1,0:T(8,128)(2,1)} async-done(((bf16[512,1536]{1,0:T(8,128)(2,1)}), bf16[8192,1536]{1,0:T(8,128)(2,1)}) %all-gather.2.cloned.1.call-update) | async-done | bytes 25165840 | tf_op jit(solution)/shard_map/all_gather | solution.py:13
  140.9 22.4 %gather_fusion.2 = bf16[96,128,1536]{2,1,0:T(8,128)(2,1)} fusion(bf16[64,128,1536]{2,1,0:T(8,128)(2,1)} %bitcast.65, s32[1024]{0:T(1024)S(1)} %get-tuple-element.11), kind=kCustom, calls=%fused_computation.2 | custom fusion | bytes 75497856 | tf_op jit(solution)/shard_map/jit(_take)/gather | solution.py:24
  163.3 0.0 copy-start
  163.3 27.5 %fusion.5 = f32[96,128,128]{2,1,0:T(8,128)} fusion(bf16[96,128,1536]{2,1,0:T(8,128)(2,1)} %gather_fusion.3, bf16[96,128,1536]{2,1,0:T(8,128)(2,1)} %gather_fusion.2, pred[96]{0:T(512)(128)(4,1)S(1)} %get-tuple-element.7, pred[96]{0:T(512)(128)(4,1)S(1)} %get-tuple-element.6), kind=kOutput, calls=%fused_computation.9 | convolution fusion | flops 4869586944 | bytes 81789120 | tf_op jit(solution)/shard_map/gqc,gdc->gqd/dot_general | solution.py:26
  190.8 0.0 reduce-scatter.5.cloned.1.call-update
  190.8 0.0 reduce-scatter.3.cloned.1.call-start
  190.9 0.0 copy-done
  190.9 5.8 %broadcast_select_fusion = bf16[16,128,1536]{2,1,0:T(8,128)(2,1)} fusion(bf16[16,128,1536]{2,1,0:T(8,128)(2,1)} %bitcast.68, pred[1536]{0:T(1024)(128)(4,1)S(1)} %add_compare_fusion), kind=kLoop, calls=%fused_computation.16 | loop fusion | flops 3145728 | bytes 12584448 | tf_op jit(solution)/shard_map/jit(_where)/select_n | solution.py:19
  196.7 23.6 %gather_fusion.1 = bf16[144,128,1536]{2,1,0:T(8,128)(2,1)} fusion(bf16[16,128,1536]{2,1,0:T(8,128)(2,1)} %broadcast_select_fusion, s32[1024]{0:T(1024)S(1)} %pad_clamp_fusion.2), kind=kCustom, calls=%fused_computation.1 | custom fusion | bytes 113246784 | tf_op jit(solution)/shard_map/jit(_take)/gather | solution.py:25
  220.3 28.6 %gather_fusion = bf16[144,128,1536]{2,1,0:T(8,128)(2,1)} fusion(bf16[64,128,1536]{2,1,0:T(8,128)(2,1)} %bitcast.66, s32[1024]{0:T(1024)S(1)} %pad_clamp_fusion.3), kind=kCustom, calls=%fused_computation | custom fusion | bytes 113246784 | tf_op jit(solution)/shard_map/jit(_take)/gather | solution.py:24
  248.8 41.7 %fusion = f32[144,128,128]{2,1,0:T(8,128)} fusion(bf16[144,128,1536]{2,1,0:T(8,128)(2,1)} %gather_fusion.1, bf16[144,128,1536]{2,1,0:T(8,128)(2,1)} %gather_fusion, pred[144]{0:T(512)(128)(4,1)S(1)} %get-tuple-element.5, pred[144]{0:T(512)(128)(4,1)S(1)} %get-tuple-element.4), kind=kOutput, calls=%fused_computation.4 | convolution fusion | flops 7304380416 | bytes 122683680 | tf_op jit(solution)/shard_map/gqc,gdc->gqd/dot_general | solution.py:26
  290.6 0.0 reduce-scatter.3.cloned.1.call-update
  291.9 0.0 reduce-scatter.5.cloned.1.call-done
  291.9 4.0 select_bitcast_fusion.1
  295.9 105.9 %reduce-scatter.3.cloned.1.call-done = f32[144,64,128]{2,1,0:T(8,128)} async-done(((f32[144,128,128]{2,1,0:T(8,128)}), f32[144,64,128]{2,1,0:T(8,128)}) %reduce-scatter.3.cloned.1.call-update) | async-done | bytes 4718608 | tf_op jit(solution)/shard_map/reduce_scatter | solution.py:36
  401.8 5.1 %select_bitcast_fusion = f32[1,144,64,128]{3,2,1,0:T(8,128)} fusion(f32[144,64,128]{2,1,0:T(8,128)} %reduce-scatter.3.cloned.1.call-done, pred[144]{0:T(512)(128)(4,1)S(1)} %iota_compare_fusion), kind=kLoop, calls=%fused_computation.17 | loop fusion | flops 2359296 | bytes 9437328 | tf_op jit(solution)/shard_map/broadcast_in_dim | solution.py:46
  (10 shorter events, 0.1 us)
Async XLA Ops:
  7.2 133.8 %all-gather.2.cloned.1.call-start = ((), (), s32[]{:S(2)}) async-start(), calls=%async_computation.2 | async-start | bytes 26738688 | tf_op jit(solution)/shard_map/all_gather | solution.py:13
  7.9 284.0 %reduce-scatter.5.cloned.1.call-start = ((), (), s32[]{:S(2)}) async-start(), calls=%async_computation.4 | async-start | bytes 9437184 | tf_op jit(solution)/shard_map/reduce_scatter | solution.py:37
  8.6 17.8 %copy-start.1 = (s32[1,96]{1,0:T(1,128)S(1)}, s32[1,96]{1,0:T(1,128)}, u32[]{:S(2)}) copy-start(s32[1,96]{1,0:T(1,128)} %param.10) | copy-start | bytes 1156
  163.3 27.6 %copy-start = (s32[1,144]{1,0:T(1,128)S(1)}, s32[1,144]{1,0:T(1,128)}, u32[]{:S(2)}) copy-start(s32[1,144]{1,0:T(1,128)} %param.8) | copy-start | bytes 1732
  190.8 211.0 %reduce-scatter.3.cloned.1.call-start = ((), (), s32[]{:S(2)}) async-start(), calls=%async_computation.3 | async-start | bytes 14155776 | tf_op jit(solution)/shard_map/reduce_scatter | solution.py:36
Sparse Core Ops, SparseCore 0:
  9.6 131.2 all-gather.1
  190.9 77.0 reduce-scatter.4
  290.7 111.0 reduce-scatter.2
where the time goes:
time: 414 us; the launch traced here: 413 us
  waiting for transfers between devices  221 us (53%)
  local copies, waits for them, and re-layouts  92.3 us (22%)
  matrix products  69.2 us (17%)
  other arithmetic  15.6 us (4%)
  between operations  15.1 us (4%)
    all_gather x1, waiting for transfers between devices, shards(): every_query = lax.all_gather(queries, 'docs', axis=0, tiled=True)  114 us
    reduce_scatter x1, waiting for transfers between devices, shards(): lax.psum_scatter(prefix_terms, 'dims', scatter_dimension=1, tiled=True)  106 us
    dot_general x2, matrix products, pair_products(): jnp.einsum('gqc,gdc->gqd', picked_queries, picked_docs, preferred_element...  69.2 us
    gather x2, local copies, waits for them, and re-layouts, pair_products(): picked_queries = jnp.take(query_blocks, pair_ids // local_blocks, axis=0)  51 us
    gather x2, local copies, waits for them, and re-layouts, pair_products(): picked_docs = jnp.take(doc_side, pair_ids % local_blocks, axis=0)  41.3 us
    broadcast_in_dim x2, other arithmetic, shards(): return (prefix_out[None], full_out[None])  9.06 us
  transfers between devices with their start and end apart: 3, of which 2 were waited for; matrix products, arithmetic and copies ran while one was open for 30% of the time, Pallas kernels for 0%

commit v1 on v0

v1 whole, which is shorter than its diff:
```python
import functools

import jax
import jax.numpy as jnp
from jax import lax
from jax.experimental import pallas as pl
from jax.experimental.pallas import tpu as pltpu
from jax.sharding import PartitionSpec as P

D = 3072
PREFIX = 768
QB = 128
DB = 128
STEPS = 12


def scores(
    n_dims, local_blocks, surv_ref, surv_n_ref, short_ref, short_n_ref, *refs
):
    query_hbm, doc_hbm = refs[:n_dims], refs[n_dims : 2 * n_dims]
    prefix_ref, full_ref, query_vmem, doc_vmem, query_sem, doc_sem = refs[2 * n_dims :]
    width = doc_vmem.shape[-1]
    step = pl.program_id(0)
    me = lax.axis_index("dims")

    @pl.when(step == 0)
    def _():
        copies = []
        for shift in range(n_dims):
            place = lax.rem(me - shift + n_dims, n_dims)
            copies.append(
                pltpu.make_async_copy(doc_hbm[shift], doc_vmem.at[place], doc_sem.at[shift])
            )
            copies.append(
                pltpu.make_async_copy(query_hbm[shift], query_vmem.at[place], query_sem.at[shift])
            )
        for copy in copies:
            copy.start()
        for copy in copies:
            copy.wait()

    def slots(pair_ref, count_ref, out_ref, columns):
        per_step = out_ref.shape[0]
        for i in range(per_step):
            slot = step * per_step + i
            pair = pair_ref[slot]
            query_block = pair // local_blocks
            doc_block = pair % local_blocks
            total = None
            for j in range(n_dims):
                used = min(max(columns - j * width, 0), width)
                if used == 0:
                    continue
                term = lax.dot_general(
                    query_vmem[j, query_block, :, :used],
                    doc_vmem[j, doc_block, :, :used],
                    (((1,), (1,)), ((), ())),
                    preferred_element_type=jnp.float32,
                )
                total = term if total is None else total + term
            scaled = total * (float(columns) ** -0.5)
            out_ref[i] = jnp.where(slot < count_ref[0], scaled, jnp.float32(0.0))

    slots(short_ref, short_n_ref, full_ref, D)
    slots(surv_ref, surv_n_ref, prefix_ref, PREFIX)


def shards(
    n_dims, queries, doc_vectors, surv_pairs, surv_count, short_pairs, short_count
):
    width = queries.shape[1]
    rows = QB // n_dims
    local_blocks = doc_vectors.shape[0] // DB
    me = lax.axis_index("dims")
    by_rows = queries.reshape(-1, n_dims, rows, width)
    docs = doc_vectors.reshape(local_blocks, DB, width)
    query_parts, doc_parts = [], []
    for shift in range(n_dims):
        target = lax.rem(me + shift, n_dims)
        part = lax.dynamic_index_in_dim(by_rows, target, 1, keepdims=False)
        doc_part = docs
        if shift:
            pairs = [(i, (i + shift) % n_dims) for i in range(n_dims)]
            part = lax.ppermute(part, "dims", pairs)
            doc_part = lax.ppermute(docs, "dims", pairs)
        query_parts.append(lax.all_gather(part, "docs", axis=0, tiled=True))
        doc_parts.append(doc_part)
    blocks = query_parts[0].shape[0]
    survivors, shortlist = surv_pairs.shape[1], short_pairs.shape[1]
    outs = [
        jax.ShapeDtypeStruct((survivors, rows, DB), jnp.float32),
        jax.ShapeDtypeStruct((shortlist, rows, DB), jnp.float32),
    ]
    moved = 2 * (blocks * rows + local_blocks * DB) * D + 4 * (survivors + shortlist) * rows * DB
    prefix_out, full_out = pl.pallas_call(
        functools.partial(scores, n_dims, local_blocks),
        out_shape=outs,
        grid_spec=pltpu.PrefetchScalarGridSpec(
            num_scalar_prefetch=4,
            grid=(STEPS,),
            in_specs=[pl.BlockSpec(memory_space=pl.ANY)] * (2 * n_dims),
            out_specs=[
                pl.BlockSpec((survivors // STEPS, rows, DB), lambda g, *_: (g, 0, 0)),
                pl.BlockSpec((shortlist // STEPS, rows, DB), lambda g, *_: (g, 0, 0)),
            ],
            scratch_shapes=[
                pltpu.VMEM((n_dims, blocks, rows, width), jnp.bfloat16),
                pltpu.VMEM((n_dims, local_blocks, DB, width), jnp.bfloat16),
                pltpu.SemaphoreType.DMA((n_dims,)),
                pltpu.SemaphoreType.DMA((n_dims,)),
            ],
        ),
        compiler_params=pltpu.CompilerParams(vmem_limit_bytes=56 * 2**20),
        cost_estimate=pl.CostEstimate(
            flops=2 * rows * DB * (shortlist * D + survivors * PREFIX),
            bytes_accessed=moved,
            transcendentals=0,
        ),
    )(surv_pairs[0], surv_count, short_pairs[0], short_count, *query_parts, *doc_parts)
    return (prefix_out[None], full_out[None])


def solution(mesh):
    placed = (
        P("docs", "dims"),
        P("docs", "dims"),
        P("docs", None),
        P("docs"),
        P("docs", None),
        P("docs"),
    )
    return jax.shard_map(
        functools.partial(shards, mesh.shape["dims"]),
        mesh=mesh,
        in_specs=placed,
        out_specs=(P("docs", None, "dims", None), P("docs", None, "dims", None)),
        check_vma=False,
    )
```

time: 414 us -> 274 us (0.66)
  local copies, waits for them, and re-layouts: 92.3 us -> 3.28 us
  matrix products: 69.2 us -> 0 us
  Pallas kernels: 0 us -> 50.7 us
  waiting for transfers between devices: 221 us -> 199 us
  other arithmetic: 15.6 us -> 0 us
  starting transfers between devices: 0.12 us -> 4.92 us
    ppermute x0 -> x2, waiting for transfers between devices: none -> 152 us  [the longest x1 134 us: shards(): doc_part = lax.ppermute(docs, 'dims', pairs)]
    reduce_scatter x2 -> x0, waiting for transfers between devices: 106 us -> none  [the longest x1 106 us: shards(): lax.psum_scatter(prefix_terms, 'dims', scatter_dimension=1, tiled=True)]
    gather x4 -> x0, local copies, waits for them, and re-layouts: 92.3 us -> none  [the longest x2 51 us: pair_products(): picked_queries = jnp.take(query_blocks, pair_ids // local_blocks, axis=0)]
    dot_general x2 -> x0, matrix products: 69.2 us -> none  [pair_products(): jnp.einsum('gqc,gdc->gqd', picked_queries, picked_docs, preferred_element...]
    all_gather x1 -> x2, waiting for transfers between devices: 114 us -> 47.8 us  [shards(): query_parts.append(lax.all_gather(part, 'docs', axis=0, tiled=True))]
    pallas_call x0 -> x1, Pallas kernels: none -> 50.7 us  [shards(): pl.pallas_call(functools.partial(scores, n_dims, local_blocks), out_shape...]
    broadcast_in_dim x2 -> x0, other arithmetic: 9.06 us -> none  [shards(): return (prefix_out[None], full_out[None])]
    select_n x4 -> x0, other arithmetic: 6.45 us -> none  [the longest x1 5.76 us: shards(): jnp.where(columns[None, None, :] < PREFIX, doc_blocks, jnp.zeros((), doc_...]
  transfers between devices with their start and end apart: 3 -> 4, of which waited for: 2 -> 3; matrix products, arithmetic and copies ran while one was open for 30% -> 0% of each run, Pallas kernels for 0% -> 0%
where the time goes in v1:
time: 274 us
  waiting for transfers between devices  199 us (73%)
  Pallas kernels  50.7 us (19%)
  between operations  15.4 us (6%)
  starting transfers between devices  4.92 us (2%)
  local copies, waits for them, and re-layouts  3.28 us (1%)
    ppermute x1, waiting for transfers between devices, shards(): doc_part = lax.ppermute(docs, 'dims', pairs)  134 us
    pallas_call x1, Pallas kernels, shards(): pl.pallas_call(functools.partial(scores, n_dims, local_blocks), out_shape...  50.7 us
    all_gather x2, waiting for transfers between devices, shards(): query_parts.append(lax.all_gather(part, 'docs', axis=0, tiled=True))  47.8 us
    ppermute x1, waiting for transfers between devices, shards(): part = lax.ppermute(part, 'dims', pairs)  17.5 us
  transfers between devices with their start and end apart: 4, of which 3 were waited for; matrix products, arithmetic and copies ran while one was open for 0% of the time, Pallas kernels for 0%

profile of v1, /device:TPU:0, one launch (start us, length us, event | category | flops | bytes accessed | tf_op | source)
XLA Modules:
  0.0 273.7 jit_solution(14004621821181278735)
XLA Ops:
  7.2 0.0 all-gather.6.cloned.1.call-start
  7.2 2.4 dynamic-slice_bitcast_fusion
  9.6 0.0 all-gather.6.cloned.1.call-update
  9.6 0.0 all-gather.4.cloned.1.call-start
  9.7 3.0 %collective-permute-start = (bf16[4,64,1536]{2,1,0:T(8,128)(2,1)S(1)}, bf16[4,64,1536]{2,1,0:T(8,128)(2,1)S(1)}, u32[]{:S(2)}, u32[]{:S(2)}) collective-permute-start(bf16[4,64,1536]{2,1,0:T(8,128)(2,1)S(1)} %get-tuple-element.6), channel_id=1, source_target_pairs={{0,1},{1,0},{2,3},{3,2},{4,5},{5,4},{6,7},{7,6},{8,9},{9,8},{10,11... | collective-permute-start | bytes 2359304 | tf_op jit(solution)/shard_map/ppermute | solution.py:84
  12.7 17.5 %collective-permute-done = bf16[4,64,1536]{2,1,0:T(8,128)(2,1)S(1)} collective-permute-done((bf16[4,64,1536]{2,1,0:T(8,128)(2,1)S(1)}, bf16[4,64,1536]{2,1,0:T(8,128)(2,1)S(1)}, u32[]{:S(2)}, u32[]{:S(2)}) %collective-permute-start) | collective-permute-done | bytes 786464 | tf_op jit(solution)/shard_map/ppermute | solution.py:84
  30.3 0.0 copy-start
  30.3 0.9 copy-done
  31.1 0.0 all-gather.4.cloned.1.call-update
  31.2 1.8 collective-permute-start.1
  34.3 134.1 %collective-permute-done.1.refs_3_ = bf16[16,128,1536]{2,1,0:T(8,128)(2,1)} collective-permute-done((bf16[16,128,1536]{2,1,0:T(8,128)(2,1)}, bf16[16,128,1536]{2,1,0:T(8,128)(2,1)}, u32[]{:S(2)}, u32[]{:S(2)}) %collective-permute-start.1) | collective-permute-done | bytes 6291488 | tf_op jit(solution)/shard_map/ppermute | solution.py:85
  168.4 0.0 all-gather.6.cloned.1.call-done
  168.4 47.8 %all-gather.4.cloned.1.call-done.refs_1_ = bf16[64,64,1536]{2,1,0:T(8,128)(2,1)} async-done(((bf16[4,64,1536]{2,1,0:T(8,128)(2,1)}), bf16[64,64,1536]{2,1,0:T(8,128)(2,1)}) %all-gather.4.cloned.1.call-update) | async-done | bytes 12582928 | tf_op jit(solution)/shard_map/all_gather | solution.py:86
  216.2 50.7 %shard_map.77 = (f32[144,64,128]{2,1,0:T(8,128)}, f32[96,64,128]{2,1,0:T(8,128)}) custom-call(s32[144]{0:T(256)} %bitcast.13, s32[1]{0:T(128)S(6)} %copy.9.surv_n_ref, s32[96]{0:T(128)} %bitcast.14, s32[1]{0:T(128)S(6)} %copy.10.short_n_ref, bf16[64,64,1536]{2,1,0:T(8,128)(2,1)} %bitcast.9, bf16[64,64,1536]{2,1,0:T(8,128)(2,1)} %all-gather.4.cloned.1.call-done.refs_1_, ...), custom_call_target="tpu_custom_call" | custom-call | flops 6643777536 | bytes 45613056 | tf_op jit(solution)/shard_map/pallas_call | solution.py:95
Async XLA Ops:
  7.2 161.2 %all-gather.6.cloned.1.call-start = ((), (), s32[]{:S(2)}) async-start(), calls=%async_computation.1 | async-start | bytes 13369344 | tf_op jit(solution)/shard_map/all_gather | solution.py:86
  9.6 206.5 %all-gather.4.cloned.1.call-start = ((), (), s32[]{:S(2)}) async-start(), calls=%async_computation | async-start | bytes 13369344 | tf_op jit(solution)/shard_map/all_gather | solution.py:86
  9.7 20.6 %collective-permute-start = (bf16[4,64,1536]{2,1,0:T(8,128)(2,1)S(1)}, bf16[4,64,1536]{2,1,0:T(8,128)(2,1)S(1)}, u32[]{:S(2)}, u32[]{:S(2)}) collective-permute-start(bf16[4,64,1536]{2,1,0:T(8,128)(2,1)S(1)} %get-tuple-element.6), channel_id=1, source_target_pairs={{0,1},{1,0},{2,3},{3,2},{4,5},{5,4},{6,7},{7,6},{8,9},{9,8},{10,11... | collective-permute-start | bytes 2359304 | tf_op jit(solution)/shard_map/ppermute | solution.py:84
  30.3 0.9 copy-start
  31.2 137.2 %collective-permute-start.1 = (bf16[16,128,1536]{2,1,0:T(8,128)(2,1)}, bf16[16,128,1536]{2,1,0:T(8,128)(2,1)}, u32[]{:S(2)}, u32[]{:S(2)}) collective-permute-start(bf16[16,128,1536]{2,1,0:T(8,128)(2,1)} %bitcast.10), channel_id=1, source_target_pairs={{0,1},{1,0},{2,3},{3,2},{4,5},{5,4},{6,7},{7,6},{8,9},{9,8},{10,11... | collective-permute-start | bytes 18874376 | tf_op jit(solution)/shard_map/ppermute | solution.py:85
Sparse Core Ops, SparseCore 0:
  10.9 103.4 all-gather.5
  117.2 98.9 all-gather.3

commit v2 on v1

--- a/solution.py
+++ b/solution.py
@@ -17,9 +17,10 @@
 def scores(
     n_dims, local_blocks, surv_ref, surv_n_ref, short_ref, short_n_ref, *refs
 ):
-    query_hbm, doc_hbm = refs[:n_dims], refs[n_dims : 2 * n_dims]
-    prefix_ref, full_ref, query_vmem, doc_vmem, query_sem, doc_sem = refs[2 * n_dims :]
+    query_hbm, doc_hbm = refs[0], refs[1 : 1 + n_dims]
+    prefix_ref, full_ref, query_vmem, doc_vmem, query_sem, doc_sem = refs[1 + n_dims :]
     width = doc_vmem.shape[-1]
+    per_shard = query_vmem.shape[2]
     step = pl.program_id(0)
     me = lax.axis_index("dims")
 
@@ -32,7 +33,9 @@
                 pltpu.make_async_copy(doc_hbm[shift], doc_vmem.at[place], doc_sem.at[shift])
             )
             copies.append(
-                pltpu.make_async_copy(query_hbm[shift], query_vmem.at[place], query_sem.at[shift])
+                pltpu.make_async_copy(
+                    query_hbm.at[:, shift], query_vmem.at[place], query_sem.at[shift]
+                )
             )
         for copy in copies:
             copy.start()
@@ -52,7 +55,7 @@
                 if used == 0:
                     continue
                 term = lax.dot_general(
-                    query_vmem[j, query_block, :, :used],
+                    query_vmem[j, query_block // per_shard, query_block % per_shard, :, :used],
                     doc_vmem[j, doc_block, :, :used],
                     (((1,), (1,)), ((), ())),
                     preferred_element_type=jnp.float32,
@@ -83,9 +86,11 @@
             pairs = [(i, (i + shift) % n_dims) for i in range(n_dims)]
             part = lax.ppermute(part, "dims", pairs)
             doc_part = lax.ppermute(docs, "dims", pairs)
-        query_parts.append(lax.all_gather(part, "docs", axis=0, tiled=True))
+        query_parts.append(part)
         doc_parts.append(doc_part)
-    blocks = query_parts[0].shape[0]
+    every_query = lax.all_gather(jnp.stack(query_parts), "docs", axis=0, tiled=False)
+    n_docs, _, per_shard = every_query.shape[:3]
+    blocks = n_docs * per_shard
     survivors, shortlist = surv_pairs.shape[1], short_pairs.shape[1]
     outs = [
         jax.ShapeDtypeStruct((survivors, rows, DB), jnp.float32),
@@ -98,13 +103,13 @@
         grid_spec=pltpu.PrefetchScalarGridSpec(
             num_scalar_prefetch=4,
             grid=(STEPS,),
-            in_specs=[pl.BlockSpec(memory_space=pl.ANY)] * (2 * n_dims),
+            in_specs=[pl.BlockSpec(memory_space=pl.ANY)] * (1 + n_dims),
             out_specs=[
                 pl.BlockSpec((survivors // STEPS, rows, DB), lambda g, *_: (g, 0, 0)),
                 pl.BlockSpec((shortlist // STEPS, rows, DB), lambda g, *_: (g, 0, 0)),
             ],
             scratch_shapes=[
-                pltpu.VMEM((n_dims, blocks, rows, width), jnp.bfloat16),
+                pltpu.VMEM((n_dims, n_docs, per_shard, rows, width), jnp.bfloat16),
                 pltpu.VMEM((n_dims, local_blocks, DB, width), jnp.bfloat16),
                 pltpu.SemaphoreType.DMA((n_dims,)),
                 pltpu.SemaphoreType.DMA((n_dims,)),
@@ -116,7 +121,7 @@
             bytes_accessed=moved,
             transcendentals=0,
         ),
-    )(surv_pairs[0], surv_count, short_pairs[0], short_count, *query_parts, *doc_parts)
+    )(surv_pairs[0], surv_count, short_pairs[0], short_count, every_query, *doc_parts)
     return (prefix_out[None], full_out[None])
 
 

time: 274 us -> 225 us (0.82)
  waiting for transfers between devices: 199 us -> 152 us
    all_gather x2 -> x1, waiting for transfers between devices: 47.8 us -> 0.01 us  [shards(): lax.all_gather(jnp.stack(query_parts), 'docs', axis=0, tiled=False)]
  transfers between devices with their start and end apart: 4 -> 3, of which waited for: 3 -> 2; matrix products, arithmetic and copies ran while one was open for 0% -> 0% of each run, Pallas kernels for 0% -> 0%
where the time goes in v2:
time: 225 us
  waiting for transfers between devices  152 us (68%)
  Pallas kernels  50.6 us (22%)
  between operations  15.4 us (7%)
  starting transfers between devices  4.88 us (2%)
    ppermute x1, waiting for transfers between devices, shards(): doc_part = lax.ppermute(docs, 'dims', pairs)  134 us
    pallas_call x1, Pallas kernels, shards(): pl.pallas_call(functools.partial(scores, n_dims, local_blocks), out_shape...  50.6 us
    ppermute x1, waiting for transfers between devices, shards(): part = lax.ppermute(part, 'dims', pairs)  17.5 us
  transfers between devices with their start and end apart: 3, of which 2 were waited for; matrix products, arithmetic and copies ran while one was open for 0% of the time, Pallas kernels for 0%

profile of v2, /device:TPU:0, one launch (start us, length us, event | category | flops | bytes accessed | tf_op | source)
XLA Modules:
  0.0 225.1 jit_solution(1023804021894576184)
XLA Ops:
  7.2 0.0 all-gather.3.cloned.1.call-start
  7.2 1.5 dynamic-slice_bitcast_fusion.1
  8.7 3.0 %collective-permute-start = (bf16[4,64,1536]{2,1,0:T(8,128)(2,1)S(1)}, bf16[4,64,1536]{2,1,0:T(8,128)(2,1)S(1)}, u32[]{:S(2)}, u32[]{:S(2)}) collective-permute-start(bf16[4,64,1536]{2,1,0:T(8,128)(2,1)S(1)} %get-tuple-element.7), channel_id=1, source_target_pairs={{0,1},{1,0},{2,3},{3,2},{4,5},{5,4},{6,7},{7,6},{8,9},{9,8},{10,11... | collective-permute-start | bytes 2359304 | tf_op jit(solution)/shard_map/ppermute | solution.py:87
  11.7 17.5 %collective-permute-done = bf16[4,64,1536]{2,1,0:T(8,128)(2,1)S(1)} collective-permute-done((bf16[4,64,1536]{2,1,0:T(8,128)(2,1)S(1)}, bf16[4,64,1536]{2,1,0:T(8,128)(2,1)S(1)}, u32[]{:S(2)}, u32[]{:S(2)}) %collective-permute-start) | collective-permute-done | bytes 786464 | tf_op jit(solution)/shard_map/ppermute | solution.py:87
  29.3 1.3 pad_maximum_fusion
  30.6 0.0 all-gather.3.cloned.1.call-update
  30.6 1.8 collective-permute-start.1
  33.7 134.0 %collective-permute-done.1.refs_2_ = bf16[16,128,1536]{2,1,0:T(8,128)(2,1)} collective-permute-done((bf16[16,128,1536]{2,1,0:T(8,128)(2,1)}, bf16[16,128,1536]{2,1,0:T(8,128)(2,1)}, u32[]{:S(2)}, u32[]{:S(2)}) %collective-permute-start.1) | collective-permute-done | bytes 6291488 | tf_op jit(solution)/shard_map/ppermute | solution.py:88
  167.7 0.0 all-gather.3.cloned.1.call-done
  167.7 50.6 %shard_map.77 = (f32[144,64,128]{2,1,0:T(8,128)}, f32[96,64,128]{2,1,0:T(8,128)}) custom-call(s32[144]{0:T(256)} %bitcast.21, s32[1]{0:T(128)S(6)} %copy.12.surv_n_ref, s32[96]{0:T(128)} %bitcast.22, s32[1]{0:T(128)S(6)} %copy.13.short_n_ref, bf16[16,2,4,64,1536]{4,3,2,1,0:T(8,128)(2,1)} %bitcast.16, bf16[16,128,1536]{2,1,0:T(8,128)(2,1)} %bitcast.18, ...), custom_call_target="tpu_custom_call" | custom-call | flops 6643777536 | bytes 45613056 | tf_op jit(solution)/shard_map/pallas_call | solution.py:100
Async XLA Ops:
  7.2 160.5 %all-gather.3.cloned.1.call-start = ((), (), s32[]{:S(2)}) async-start(), calls=%async_computation | async-start | bytes 26738688 | tf_op jit(solution)/shard_map/all_gather | solution.py:91
  8.7 20.6 %collective-permute-start = (bf16[4,64,1536]{2,1,0:T(8,128)(2,1)S(1)}, bf16[4,64,1536]{2,1,0:T(8,128)(2,1)S(1)}, u32[]{:S(2)}, u32[]{:S(2)}) collective-permute-start(bf16[4,64,1536]{2,1,0:T(8,128)(2,1)S(1)} %get-tuple-element.7), channel_id=1, source_target_pairs={{0,1},{1,0},{2,3},{3,2},{4,5},{5,4},{6,7},{7,6},{8,9},{9,8},{10,11... | collective-permute-start | bytes 2359304 | tf_op jit(solution)/shard_map/ppermute | solution.py:87
  30.6 137.1 %collective-permute-start.1 = (bf16[16,128,1536]{2,1,0:T(8,128)(2,1)}, bf16[16,128,1536]{2,1,0:T(8,128)(2,1)}, u32[]{:S(2)}, u32[]{:S(2)}) collective-permute-start(bf16[16,128,1536]{2,1,0:T(8,128)(2,1)} %bitcast.17), channel_id=1, source_target_pairs={{0,1},{1,0},{2,3},{3,2},{4,5},{5,4},{6,7},{7,6},{8,9},{9,8},{10,11... | collective-permute-start | bytes 18874376 | tf_op jit(solution)/shard_map/ppermute | solution.py:88
Sparse Core Ops, SparseCore 0:
  30.7 130.0 all-gather.2

commit v3 on v2

--- a/solution.py
+++ b/solution.py
@@ -11,7 +11,7 @@
 PREFIX = 768
 QB = 128
 DB = 128
-STEPS = 12
+STEPS = 6
 
 
 def scores(
@@ -24,28 +24,46 @@
     step = pl.program_id(0)
     me = lax.axis_index("dims")
 
+    early = [j for j in range(n_dims) if j * width < PREFIX]
+    late = [j for j in range(n_dims) if j * width >= PREFIX]
+
+    def query_copy(j):
+        shift = lax.rem(me - j + n_dims, n_dims)
+        return pltpu.make_async_copy(
+            query_hbm.at[:, shift], query_vmem.at[j], query_sem.at[j]
+        )
+
+    def doc_copy(j, shift):
+        return pltpu.make_async_copy(doc_hbm[shift], doc_vmem.at[j], doc_sem.at[j])
+
+    def start(places):
+        for j in places:
+            query_copy(j).start()
+            for shift in range(n_dims):
+
+                @pl.when(lax.rem(me - j + n_dims, n_dims) == shift)
+                def _(j=j, shift=shift):
+                    doc_copy(j, shift).start()
+
+    def wait(places):
+        for j in places:
+            query_copy(j).wait()
+            doc_copy(j, 0).wait()
+
     @pl.when(step == 0)
     def _():
-        copies = []
-        for shift in range(n_dims):
-            place = lax.rem(me - shift + n_dims, n_dims)
-            copies.append(
-                pltpu.make_async_copy(doc_hbm[shift], doc_vmem.at[place], doc_sem.at[shift])
-            )
-            copies.append(
-                pltpu.make_async_copy(
-                    query_hbm.at[:, shift], query_vmem.at[place], query_sem.at[shift]
-                )
-            )
-        for copy in copies:
-            copy.start()
-        for copy in copies:
-            copy.wait()
+        start(early)
+        wait(early)
+        start(late)
 
-    def slots(pair_ref, count_ref, out_ref, columns):
+    @pl.when(step == STEPS)
+    def _():
+        wait(late)
+
+    def slots(at, pair_ref, count_ref, out_ref, columns):
         per_step = out_ref.shape[0]
         for i in range(per_step):
-            slot = step * per_step + i
+            slot = at * per_step + i
             pair = pair_ref[slot]
             query_block = pair // local_blocks
             doc_block = pair % local_blocks
@@ -64,8 +82,13 @@
             scaled = total * (float(columns) ** -0.5)
             out_ref[i] = jnp.where(slot < count_ref[0], scaled, jnp.float32(0.0))
 
-    slots(short_ref, short_n_ref, full_ref, D)
-    slots(surv_ref, surv_n_ref, prefix_ref, PREFIX)
+    @pl.when(step < STEPS)
+    def _():
+        slots(step, surv_ref, surv_n_ref, prefix_ref, PREFIX)
+
+    @pl.when(step >= STEPS)
+    def _():
+        slots(step - STEPS, short_ref, short_n_ref, full_ref, D)
 
 
 def shards(
@@ -102,11 +125,11 @@
         out_shape=outs,
         grid_spec=pltpu.PrefetchScalarGridSpec(
             num_scalar_prefetch=4,
-            grid=(STEPS,),
+            grid=(2 * STEPS,),
             in_specs=[pl.BlockSpec(memory_space=pl.ANY)] * (1 + n_dims),
             out_specs=[
-                pl.BlockSpec((survivors // STEPS, rows, DB), lambda g, *_: (g, 0, 0)),
-                pl.BlockSpec((shortlist // STEPS, rows, DB), lambda g, *_: (g, 0, 0)),
+                pl.BlockSpec((survivors // STEPS, rows, DB), lambda g, *_: (jnp.minimum(g, STEPS - 1), 0, 0)),
+                pl.BlockSpec((shortlist // STEPS, rows, DB), lambda g, *_: (jnp.maximum(g - STEPS, 0), 0, 0)),
             ],
             scratch_shapes=[
                 pltpu.VMEM((n_dims, n_docs, per_shard, rows, width), jnp.bfloat16),

time: 225 us -> 221 us (0.982)
  Pallas kernels: 50.6 us -> 45.9 us
    pallas_call x1, Pallas kernels: 50.6 us -> 45.9 us  [shards(): pl.pallas_call(functools.partial(scores, n_dims, local_blocks), out_shape...]
where the time goes in v3:
time: 221 us; the launch traced here: 220 us
  waiting for transfers between devices  152 us (69%)
  Pallas kernels  45.9 us (21%)
  between operations  15.4 us (7%)
  starting transfers between devices  4.88 us (2%)
    ppermute x1, waiting for transfers between devices, shards(): doc_part = lax.ppermute(docs, 'dims', pairs)  134 us
    pallas_call x1, Pallas kernels, shards(): pl.pallas_call(functools.partial(scores, n_dims, local_blocks), out_shape...  45.9 us
    ppermute x1, waiting for transfers between devices, shards(): part = lax.ppermute(part, 'dims', pairs)  17.5 us
  transfers between devices with their start and end apart: 3, of which 2 were waited for; matrix products, arithmetic and copies ran while one was open for 0% of the time, Pallas kernels for 0%

profile of v3, /device:TPU:0, one launch (start us, length us, event | category | flops | bytes accessed | tf_op | source)
XLA Modules:
  0.0 220.4 jit_solution(16466634999201969309)
XLA Ops:
  7.2 0.0 all-gather.3.cloned.1.call-start
  7.2 1.5 dynamic-slice_bitcast_fusion.1
  8.7 3.0 %collective-permute-start = (bf16[4,64,1536]{2,1,0:T(8,128)(2,1)S(1)}, bf16[4,64,1536]{2,1,0:T(8,128)(2,1)S(1)}, u32[]{:S(2)}, u32[]{:S(2)}) collective-permute-start(bf16[4,64,1536]{2,1,0:T(8,128)(2,1)S(1)} %get-tuple-element.7), channel_id=1, source_target_pairs={{0,1},{1,0},{2,3},{3,2},{4,5},{5,4},{6,7},{7,6},{8,9},{9,8},{10,11... | collective-permute-start | bytes 2359304 | tf_op jit(solution)/shard_map/ppermute | solution.py:110
  11.7 17.5 %collective-permute-done = bf16[4,64,1536]{2,1,0:T(8,128)(2,1)S(1)} collective-permute-done((bf16[4,64,1536]{2,1,0:T(8,128)(2,1)S(1)}, bf16[4,64,1536]{2,1,0:T(8,128)(2,1)S(1)}, u32[]{:S(2)}, u32[]{:S(2)}) %collective-permute-start) | collective-permute-done | bytes 786464 | tf_op jit(solution)/shard_map/ppermute | solution.py:110
  29.3 1.3 pad_maximum_fusion
  30.6 0.0 all-gather.3.cloned.1.call-update
  30.6 1.8 collective-permute-start.1
  33.7 134.0 %collective-permute-done.1.refs_2_ = bf16[16,128,1536]{2,1,0:T(8,128)(2,1)} collective-permute-done((bf16[16,128,1536]{2,1,0:T(8,128)(2,1)}, bf16[16,128,1536]{2,1,0:T(8,128)(2,1)}, u32[]{:S(2)}, u32[]{:S(2)}) %collective-permute-start.1) | collective-permute-done | bytes 6291488 | tf_op jit(solution)/shard_map/ppermute | solution.py:111
  167.7 0.0 all-gather.3.cloned.1.call-done
  167.7 45.9 %shard_map.77 = (f32[144,64,128]{2,1,0:T(8,128)}, f32[96,64,128]{2,1,0:T(8,128)}) custom-call(s32[144]{0:T(256)} %bitcast.21, s32[1]{0:T(128)S(6)} %copy.12.surv_n_ref, s32[96]{0:T(128)} %bitcast.22, s32[1]{0:T(128)S(6)} %copy.13.short_n_ref, bf16[16,2,4,64,1536]{4,3,2,1,0:T(8,128)(2,1)} %bitcast.16, bf16[16,128,1536]{2,1,0:T(8,128)(2,1)} %bitcast.18, ...), custom_call_target="tpu_custom_call" | custom-call | flops 6643777536 | bytes 45613056 | tf_op jit(solution)/shard_map/pallas_call | solution.py:123
Async XLA Ops:
  7.2 160.5 %all-gather.3.cloned.1.call-start = ((), (), s32[]{:S(2)}) async-start(), calls=%async_computation | async-start | bytes 26738688 | tf_op jit(solution)/shard_map/all_gather | solution.py:114
  8.7 20.6 %collective-permute-start = (bf16[4,64,1536]{2,1,0:T(8,128)(2,1)S(1)}, bf16[4,64,1536]{2,1,0:T(8,128)(2,1)S(1)}, u32[]{:S(2)}, u32[]{:S(2)}) collective-permute-start(bf16[4,64,1536]{2,1,0:T(8,128)(2,1)S(1)} %get-tuple-element.7), channel_id=1, source_target_pairs={{0,1},{1,0},{2,3},{3,2},{4,5},{5,4},{6,7},{7,6},{8,9},{9,8},{10,11... | collective-permute-start | bytes 2359304 | tf_op jit(solution)/shard_map/ppermute | solution.py:110
  30.6 137.1 %collective-permute-start.1 = (bf16[16,128,1536]{2,1,0:T(8,128)(2,1)}, bf16[16,128,1536]{2,1,0:T(8,128)(2,1)}, u32[]{:S(2)}, u32[]{:S(2)}) collective-permute-start(bf16[16,128,1536]{2,1,0:T(8,128)(2,1)} %bitcast.17), channel_id=1, source_target_pairs={{0,1},{1,0},{2,3},{3,2},{4,5},{5,4},{6,7},{7,6},{8,9},{9,8},{10,11... | collective-permute-start | bytes 18874376 | tf_op jit(solution)/shard_map/ppermute | solution.py:111
Sparse Core Ops, SparseCore 0:
  30.7 130.0 all-gather.2
